TPU v7x, 256 devices: a whole 4x4x8 slice. The times are simulated.
256 devices in a mesh: ctx: 64 (over z, x, core), head: 4 (over y).
Axes of the slice: x: 4, y: 4, z: 8, core: 2. Of those that a mesh axis runs over, the one named last changes fastest.
Arguments:
- queries: bfloat16 [8192, 4096], P('ctx', 'head'), may hold values from -40 to 40
- keys: bfloat16 [8192, 4096], P('ctx', 'head'), may hold values from -40 to 40
- values: bfloat16 [8192, 4096], P('ctx', 'head'), may hold values from -50 to 50
- pattern: int32 [64, 8], replicated, may hold values from -1 to 63, as said below
- upstream: bfloat16 [8192, 4096], P('ctx', 'head'), may hold values from -6 to 6
Outputs:
- normed: bfloat16 [8192, 4096], P('ctx', 'head')
- grad_queries: bfloat16 [8192, 4096], P('ctx', 'head')
- grad_keys: bfloat16 [8192, 4096], P('ctx', 'head')
- grad_values: bfloat16 [8192, 4096], P('ctx', 'head')
Inputs may be any that keep to these rules, and one draw needn't show every extreme that they name: `pattern`: entry [i, k] for k < 7 is either i - 2^k or -1, and always -1 where i < 2^k; entry [i, 7] is i.
All inputs are finite; a program needn't handle non-finite values.
Results may differ from a plain program's by a relative error of at most 0.04.
Values may be sent and summed in bfloat16 or wider, within the bound.
A program may use at most 64 MiB of HBM per device.

v0:
```python
import jax
import jax.numpy as jnp
from jax import lax
from jax.sharding import PartitionSpec as P

HD = 128
BLOCK = 128
LEVELS = 7
WIDTH = 4096
NEG_BIG = -1e30
EPSILON = 1e-06


def shifted(block, axis, distance):
    devices = range(lax.axis_size(axis))
    route = [(i - distance, i) for i in devices if i - distance in devices]
    return lax.ppermute(block, axis, route)


def for_sending(x):
    return jax.tree.map(lambda a: a.astype(jnp.bfloat16) if a.dtype == jnp.float32 else a, x)


def route_table(blocks, levels):
    routing = []
    for query_block in range(blocks):
        for level_index in range(levels + 1):
            if level_index == levels:
                routing.append((0, query_block))
            else:
                distance = 2**level_index
                routing.append(
                    (-((query_block - distance) // blocks), (query_block - distance) % blocks)
                )
    return routing


def pair_grads(
    query_tiles, grad_tiles, lse_tiles, delta_tiles, key_tiles, value_tiles, keep_mask, score_scale
):
    scores = (
        jnp.einsum("pqhd,pkhd->phqk", query_tiles, key_tiles, preferred_element_type=jnp.float32)
        * score_scale
    )
    scores = jnp.where(keep_mask[:, None], scores, NEG_BIG)
    weights = jnp.exp(scores - lse_tiles[..., None])
    prob_tiles = weights.astype(jnp.bfloat16)
    grad_probs = jnp.einsum(
        "pqhd,pkhd->phqk", grad_tiles, value_tiles, preferred_element_type=jnp.float32
    )
    dscore = (weights * (grad_probs - delta_tiles[..., None]) * score_scale).astype(jnp.bfloat16)
    return (dscore, prob_tiles)


def key_grads(dscore, prob_tiles, query_tiles, grad_tiles):
    key_part = jnp.einsum(
        "phqk,pqhd->pkhd", dscore, query_tiles, preferred_element_type=jnp.float32
    )
    value_part = jnp.einsum(
        "phqk,pqhd->pkhd", prob_tiles, grad_tiles, preferred_element_type=jnp.float32
    )
    return jnp.stack((key_part, value_part))


def collect(partials, targets, blocks):
    pieces = []
    for key_index in range(blocks):
        summed = jnp.zeros((2,) + partials.shape[2:], jnp.float32)
        for row_index, target in enumerate(targets):
            if target == key_index:
                summed = summed + partials[:, row_index]
        pieces.append(summed)
    return jnp.stack(pieces, axis=1)


def shards(queries, keys, values, pattern, upstream):
    tokens_here = queries.shape[0]
    heads_here = queries.shape[1] // HD
    blocks = tokens_here // BLOCK
    slot_count = LEVELS + 1
    pair_count = blocks * slot_count
    score_scale = HD ** (-0.5)
    ctx_count = lax.axis_size("ctx")
    device_index = lax.axis_index("ctx")
    routing = route_table(blocks, LEVELS)
    offsets = sorted(
        set((route_entry[0] for route_entry in routing if 0 < route_entry[0] < ctx_count))
    )
    tile_shape = (blocks, BLOCK, heads_here, HD)
    query_blocks = queries.reshape(tile_shape)
    own_pairs = jnp.stack((keys, values)).reshape((2,) + tile_shape)
    sources = {0: own_pairs}
    for offset in offsets:
        fetched = shifted(jnp.stack((keys, values)), "ctx", offset)
        sources[offset] = fetched.reshape((2,) + tile_shape)
    empty_tile = jnp.zeros((2, BLOCK, heads_here, HD), jnp.bfloat16)
    gathered = []
    for source, key_index in routing:
        if source in sources:
            gathered.append(sources[source][:, key_index])
        else:
            gathered.append(empty_tile)
    pair_kv = jnp.stack(gathered, axis=1)
    key_tiles = pair_kv[0]
    value_tiles = pair_kv[1]
    key_stack = key_tiles.reshape((blocks, slot_count) + tile_shape[1:])
    value_stack = value_tiles.reshape((blocks, slot_count) + tile_shape[1:])
    own_rows = lax.dynamic_slice_in_dim(pattern, device_index * blocks, blocks, 0)
    positions = jnp.arange(BLOCK)
    causal = positions[None, :] <= positions[:, None]
    self_slot = jnp.arange(slot_count) == LEVELS
    tile_keep = (own_rows >= 0)[:, :, None, None] & (
        jnp.logical_not(self_slot)[None, :, None, None] | causal[None, None]
    )
    scores = (
        jnp.einsum("bqhd,bskhd->bhqsk", query_blocks, key_stack, preferred_element_type=jnp.float32)
        * score_scale
    )
    scores = jnp.where(jnp.transpose(tile_keep, (0, 2, 1, 3))[:, None], scores, NEG_BIG)
    highest = jnp.max(scores, axis=(3, 4))
    log_total = highest + jnp.log(jnp.sum(jnp.exp(scores - highest[..., None, None]), axis=(3, 4)))
    prob_stack = jnp.exp(scores - log_total[..., None, None]).astype(jnp.bfloat16)
    attention = jnp.einsum(
        "bhqsk,bskhd->bqhd", prob_stack, value_stack, preferred_element_type=jnp.float32
    ).astype(jnp.bfloat16)
    attn_wide = attention.reshape(tokens_here, heads_here * HD).astype(jnp.float32)
    square_sum = lax.psum(jnp.sum(attn_wide * attn_wide, axis=1), "head")
    inverse = lax.rsqrt(square_sum / WIDTH + EPSILON)
    normed = (attn_wide * inverse[:, None]).astype(jnp.bfloat16)
    upstream_wide = upstream.astype(jnp.float32)
    cross_term = lax.psum(jnp.sum(upstream_wide * attn_wide, axis=1), "head")
    grad_attn = (
        inverse[:, None] * upstream_wide - attn_wide * (inverse**3 * cross_term / WIDTH)[:, None]
    ).astype(jnp.bfloat16)
    row_delta = jnp.sum(
        (grad_attn.astype(jnp.float32) * attn_wide).reshape(tokens_here, heads_here, HD), axis=2
    )
    row_delta = jnp.transpose(row_delta.reshape(blocks, BLOCK, heads_here), (0, 2, 1))

    def spread(array):
        return jnp.broadcast_to(array[:, None], (blocks, slot_count) + array.shape[1:]).reshape(
            (pair_count,) + array.shape[1:]
        )

    grad_blocks = grad_attn.reshape(tile_shape)
    query_pairs = spread(query_blocks)
    grad_pairs = spread(grad_blocks)
    keep_pairs = tile_keep.reshape(pair_count, BLOCK, BLOCK)
    dscore, prob_pairs = pair_grads(
        query_pairs,
        grad_pairs,
        spread(log_total),
        spread(row_delta),
        key_tiles,
        value_tiles,
        keep_pairs,
        score_scale,
    )
    grad_query = jnp.einsum(
        "phqk,pkhd->pqhd", dscore, key_tiles, preferred_element_type=jnp.float32
    )
    grad_query = jnp.sum(grad_query.reshape((blocks, slot_count) + tile_shape[1:]), axis=1)
    grad_queries = grad_query.astype(jnp.bfloat16).reshape(tokens_here, heads_here * HD)
    local_rows = [row_index for row_index in range(pair_count) if routing[row_index][0] == 0]
    chosen = jnp.array(local_rows, jnp.int32)
    local_terms = key_grads(
        dscore[chosen], prob_pairs[chosen], query_pairs[chosen], grad_pairs[chosen]
    )
    key_sum = collect(local_terms, [routing[row_index][1] for row_index in local_rows], blocks)
    for offset in offsets:
        remote_rows = [
            row_index for row_index in range(pair_count) if routing[row_index][0] == offset
        ]
        chosen = jnp.array(remote_rows, jnp.int32)
        remote_terms = key_grads(
            dscore[chosen], prob_pairs[chosen], query_pairs[chosen], grad_pairs[chosen]
        )
        outgoing = collect(
            remote_terms, [routing[row_index][1] for row_index in remote_rows], blocks
        )
        key_sum = key_sum + shifted(for_sending(outgoing), "ctx", -offset).astype(outgoing.dtype)
    grad_keys = key_sum[0].astype(jnp.bfloat16).reshape(tokens_here, heads_here * HD)
    grad_values = key_sum[1].astype(jnp.bfloat16).reshape(tokens_here, heads_here * HD)
    return (normed, grad_queries, grad_keys, grad_values)


def solution(mesh):
    return jax.shard_map(
        shards,
        mesh=mesh,
        in_specs=(P("ctx", "head"), P("ctx", "head"), P("ctx", "head"), P(), P("ctx", "head")),
        out_specs=(P("ctx", "head"), P("ctx", "head"), P("ctx", "head"), P("ctx", "head")),
        check_vma=False,
    )
```

profile of v0, /device:TPU:64, one launch (start us, length us, event | category | flops | bytes accessed | tf_op | source)
XLA Modules:
  0.0 228.5 jit_solution(5779457081914570927)
XLA Ops:
  3.0 8.1 %collective-permute-start.5 = (bf16[2,128,1024]{1,2,0:T(8,128)(2,1)S(1)}, bf16[2,128,1024]{1,2,0:T(8,128)(2,1)}, u32[]{:S(2)}, u32[]{:S(2)}) collective-permute-start(bf16[2,128,1024]{1,2,0:T(8,128)(2,1)S(1)} %pad_maximum_fusion), channel_id=1, source_target_pairs={{0,128},{4,132},{8,136},{12,140},{16,144},{20,148},{24,152},{28,15... | collective-permute-start | bytes 1572872 | tf_op jit(solution)/shard_map/ppermute | solution.py:17
  11.1 1.9 collective-permute-start.4
  13.0 2.9 %collective-permute-start.3 = (bf16[2,128,1024]{1,2,0:T(8,128)(2,1)S(1)}, bf16[2,128,1024]{1,2,0:T(8,128)(2,1)S(1)}, u32[]{:S(2)}, u32[]{:S(2)}) collective-permute-start(bf16[2,128,1024]{1,2,0:T(8,128)(2,1)S(1)} %pad_maximum_fusion), channel_id=1, source_target_pairs={{0,32},{4,36},{8,40},{12,44},{16,48},{20,52},{24,56},{28,60},{32,6... | collective-permute-start | bytes 1572872 | tf_op jit(solution)/shard_map/ppermute | solution.py:17
  15.9 4.9 %collective-permute-start.2 = (bf16[2,128,1024]{1,2,0:T(8,128)(2,1)S(1)}, bf16[2,128,1024]{1,2,0:T(8,128)(2,1)S(1)}, u32[]{:S(2)}, u32[]{:S(2)}) collective-permute-start(bf16[2,128,1024]{1,2,0:T(8,128)(2,1)S(1)} %pad_maximum_fusion), channel_id=1, source_target_pairs={{0,16},{4,20},{8,24},{12,28},{16,32},{20,36},{24,40},{28,44},{32,4... | collective-permute-start | bytes 1572872 | tf_op jit(solution)/shard_map/ppermute | solution.py:17
  20.9 2.5 %collective-permute-start.1 = (bf16[2,128,1024]{1,2,0:T(8,128)(2,1)S(1)}, bf16[2,128,1024]{1,2,0:T(8,128)(2,1)S(1)}, u32[]{:S(2)}, u32[]{:S(2)}) collective-permute-start(bf16[2,128,1024]{1,2,0:T(8,128)(2,1)S(1)} %pad_maximum_fusion), channel_id=1, source_target_pairs={{0,8},{4,12},{8,16},{12,20},{16,24},{20,28},{24,32},{28,36},{32,40... | collective-permute-start | bytes 1572872 | tf_op jit(solution)/shard_map/ppermute | solution.py:17
  24.3 10.3 %collective-permute-done.5 = bf16[2,128,1024]{1,2,0:T(8,128)(2,1)} collective-permute-done((bf16[2,128,1024]{1,2,0:T(8,128)(2,1)S(1)}, bf16[2,128,1024]{1,2,0:T(8,128)(2,1)}, u32[]{:S(2)}, u32[]{:S(2)}) %collective-permute-start.5) | collective-permute-done | bytes 524320 | tf_op jit(solution)/shard_map/ppermute | solution.py:17
  34.7 1.9 collective-permute-start
  44.5 11.9 %collective-permute-done.4 = bf16[2,128,1024]{1,2,0:T(8,128)(2,1)S(1)} collective-permute-done((bf16[2,128,1024]{1,2,0:T(8,128)(2,1)S(1)}, bf16[2,128,1024]{1,2,0:T(8,128)(2,1)S(1)}, u32[]{:S(2)}, u32[]{:S(2)}) %collective-permute-start.4) | collective-permute-done | bytes 524320 | tf_op jit(solution)/shard_map/ppermute | solution.py:17
  58.4 8.1 %collective-permute-done.3 = bf16[2,128,1024]{1,2,0:T(8,128)(2,1)S(1)} collective-permute-done((bf16[2,128,1024]{1,2,0:T(8,128)(2,1)S(1)}, bf16[2,128,1024]{1,2,0:T(8,128)(2,1)S(1)}, u32[]{:S(2)}, u32[]{:S(2)}) %collective-permute-start.3) | collective-permute-done | bytes 524320 | tf_op jit(solution)/shard_map/ppermute | solution.py:17
  68.7 2.5 %collective-permute-done.2 = bf16[2,128,1024]{1,2,0:T(8,128)(2,1)S(1)} collective-permute-done((bf16[2,128,1024]{1,2,0:T(8,128)(2,1)S(1)}, bf16[2,128,1024]{1,2,0:T(8,128)(2,1)S(1)}, u32[]{:S(2)}, u32[]{:S(2)}) %collective-permute-start.2) | collective-permute-done | bytes 524320 | tf_op jit(solution)/shard_map/ppermute | solution.py:17
  73.3 8.9 %collective-permute-done.1 = bf16[2,128,1024]{1,2,0:T(8,128)(2,1)S(1)} collective-permute-done((bf16[2,128,1024]{1,2,0:T(8,128)(2,1)S(1)}, bf16[2,128,1024]{1,2,0:T(8,128)(2,1)S(1)}, u32[]{:S(2)}, u32[]{:S(2)}) %collective-permute-start.1) | collective-permute-done | bytes 524320 | tf_op jit(solution)/shard_map/ppermute | solution.py:17
  84.3 3.5 %collective-permute-done = bf16[2,128,1024]{1,2,0:T(8,128)(2,1)} collective-permute-done((bf16[2,128,1024]{1,2,0:T(8,128)(2,1)S(1)}, bf16[2,128,1024]{1,2,0:T(8,128)(2,1)}, u32[]{:S(2)}, u32[]{:S(2)}) %collective-permute-start) | collective-permute-done | bytes 524320 | tf_op jit(solution)/shard_map/ppermute | solution.py:17
  90.3 2.0 slice_bitcast_fusion.1
  94.1 2.4 %multiply_reduce_fusion = (f32[128]{0:T(128)S(1)}, f32[8,128,128]{2,1,0:T(8,128)}) fusion(f32[8,8,128,128]{3,2,1,0:T(8,128)S(1)} %get-tuple-element.336, f32[8,128]{1,0:T(8,128)S(1)} %log_add_fusion, pred[128,8,128]{0,2,1:T(8,128)(4,1)S(1)} %and_bitcast_fusion, bf16[2,8,128,8,128]{4,2,1,3,0:T(8,128)(2,1)S(1)} %maximum_dynamic-update-slice_fusion), kind=kOutput, calls=%fused_computation.76 | convolution fusion | flops 273153920 | bytes 6951424 | tf_op jit(solution)/shard_map/bhqsk,bskhd->bqhd/dot_general | solution.py:123
  97.9 10.9 %all-reduce = (f32[128]{0:T(128)S(1)}, f32[128]{0:T(128)S(1)}) all-reduce(f32[128]{0:T(128)S(1)} %get-tuple-element.337, f32[128]{0:T(128)S(1)} %fusion.45), channel_id=1, replica_groups=mesh['ctx'=64,'head'=4] {'head'}, use_global_device_ids=true, to_apply=%region_3.4 | all-reduce | flops 256 | bytes 2048 | tf_op jit(solution)/shard_map/psum | solution.py:127
  110.2 3.3 %fusion.3 = (bf16[8,8,128,128]{3,2,1,0:T(8,128)(2,1)S(1)}, f32[8,8,128,128]{2,3,1,0:T(8,128)S(1)}) fusion(f32[8,128]{1,0:T(8,128)S(1)} %log_add_fusion, pred[8,128,128]{2,1,0:T(8,128)(4,1)S(1)} %copy-done.13, bf16[128,8,128]{2,0,1:T(8,128)(2,1)} %copy_bitcast_fusion.1, bf16[8,128,8,128]{3,1,0,2:T(8,128)(2,1)} %get-tuple-element.327), kind=kOutput, calls=%fused_computation.8 | convolution fusion | flops 272629760 | bytes 8785920 | tf_op jit(solution)/shard_map/pqhd,pkhd->phqk/dot_general | solution.py:42
  113.5 2.2 multiply_convert_fusion
  118.6 2.2 collective-permute-start.6
  121.6 1.9 collective-permute-start.7
  124.4 1.9 collective-permute-start.8
  138.7 11.2 %collective-permute-done.7 = bf16[2,1,128,8,128]{2,4,3,1,0:T(8,128)(2,1)S(1)} collective-permute-done((bf16[2,1,128,8,128]{2,4,3,1,0:T(8,128)(2,1)}, bf16[2,1,128,8,128]{2,4,3,1,0:T(8,128)(2,1)S(1)}, u32[]{:S(2)}, u32[]{:S(2)}) %collective-permute-start.7) | collective-permute-done | bytes 524320 | tf_op jit(solution)/shard_map/ppermute | solution.py:17
  149.9 11.2 %collective-permute-done.8 = bf16[2,1,128,8,128]{2,4,3,1,0:T(8,128)(2,1)S(1)} collective-permute-done((bf16[2,1,128,8,128]{2,4,3,1,0:T(8,128)(2,1)}, bf16[2,1,128,8,128]{2,4,3,1,0:T(8,128)(2,1)S(1)}, u32[]{:S(2)}, u32[]{:S(2)}) %collective-permute-start.8) | collective-permute-done | bytes 524320 | tf_op jit(solution)/shard_map/ppermute | solution.py:17
  161.1 23.4 %collective-permute-done.9 = bf16[2,1,128,8,128]{2,4,3,1,0:T(8,128)(2,1)S(1)} collective-permute-done((bf16[2,1,128,8,128]{2,4,3,1,0:T(8,128)(2,1)}, bf16[2,1,128,8,128]{2,4,3,1,0:T(8,128)(2,1)S(1)}, u32[]{:S(2)}, u32[]{:S(2)}) %collective-permute-start.9) | collective-permute-done | bytes 524320 | tf_op jit(solution)/shard_map/ppermute | solution.py:17
  184.6 40.6 %collective-permute-done.10 = bf16[2,1,128,8,128]{2,4,3,1,0:T(8,128)(2,1)S(1)} collective-permute-done((bf16[2,1,128,8,128]{2,4,3,1,0:T(8,128)(2,1)}, bf16[2,1,128,8,128]{2,4,3,1,0:T(8,128)(2,1)S(1)}, u32[]{:S(2)}, u32[]{:S(2)}) %collective-permute-start.10) | collective-permute-done | bytes 524320 | tf_op jit(solution)/shard_map/ppermute | solution.py:17
  (101 shorter events, 46.6 us)
Async XLA Ops:
  0.6 41.8 %copy-start = (bf16[128,1024]{1,0:T(8,128)(2,1)S(1)}, bf16[128,1024]{1,0:T(8,128)(2,1)}, u32[]{:S(2)}) copy-start(bf16[128,1024]{1,0:T(8,128)(2,1)} %param.12) | copy-start | bytes 786436
  3.0 31.7 %collective-permute-start.5 = (bf16[2,128,1024]{1,2,0:T(8,128)(2,1)S(1)}, bf16[2,128,1024]{1,2,0:T(8,128)(2,1)}, u32[]{:S(2)}, u32[]{:S(2)}) collective-permute-start(bf16[2,128,1024]{1,2,0:T(8,128)(2,1)S(1)} %pad_maximum_fusion), channel_id=1, source_target_pairs={{0,128},{4,132},{8,136},{12,140},{16,144},{20,148},{24,152},{28,15... | collective-permute-start | bytes 1572872 | tf_op jit(solution)/shard_map/ppermute | solution.py:17
  11.1 45.2 %collective-permute-start.4 = (bf16[2,128,1024]{1,2,0:T(8,128)(2,1)S(1)}, bf16[2,128,1024]{1,2,0:T(8,128)(2,1)S(1)}, u32[]{:S(2)}, u32[]{:S(2)}) collective-permute-start(bf16[2,128,1024]{1,2,0:T(8,128)(2,1)S(1)} %pad_maximum_fusion), channel_id=1, source_target_pairs={{0,64},{4,68},{8,72},{12,76},{16,80},{20,84},{24,88},{28,92},{32,9... | collective-permute-start | bytes 1572872 | tf_op jit(solution)/shard_map/ppermute | solution.py:17
  13.0 53.6 %collective-permute-start.3 = (bf16[2,128,1024]{1,2,0:T(8,128)(2,1)S(1)}, bf16[2,128,1024]{1,2,0:T(8,128)(2,1)S(1)}, u32[]{:S(2)}, u32[]{:S(2)}) collective-permute-start(bf16[2,128,1024]{1,2,0:T(8,128)(2,1)S(1)} %pad_maximum_fusion), channel_id=1, source_target_pairs={{0,32},{4,36},{8,40},{12,44},{16,48},{20,52},{24,56},{28,60},{32,6... | collective-permute-start | bytes 1572872 | tf_op jit(solution)/shard_map/ppermute | solution.py:17
  15.9 55.2 %collective-permute-start.2 = (bf16[2,128,1024]{1,2,0:T(8,128)(2,1)S(1)}, bf16[2,128,1024]{1,2,0:T(8,128)(2,1)S(1)}, u32[]{:S(2)}, u32[]{:S(2)}) collective-permute-start(bf16[2,128,1024]{1,2,0:T(8,128)(2,1)S(1)} %pad_maximum_fusion), channel_id=1, source_target_pairs={{0,16},{4,20},{8,24},{12,28},{16,32},{20,36},{24,40},{28,44},{32,4... | collective-permute-start | bytes 1572872 | tf_op jit(solution)/shard_map/ppermute | solution.py:17
  20.9 61.3 %collective-permute-start.1 = (bf16[2,128,1024]{1,2,0:T(8,128)(2,1)S(1)}, bf16[2,128,1024]{1,2,0:T(8,128)(2,1)S(1)}, u32[]{:S(2)}, u32[]{:S(2)}) collective-permute-start(bf16[2,128,1024]{1,2,0:T(8,128)(2,1)S(1)} %pad_maximum_fusion), channel_id=1, source_target_pairs={{0,8},{4,12},{8,16},{12,20},{16,24},{20,28},{24,32},{28,36},{32,40... | collective-permute-start | bytes 1572872 | tf_op jit(solution)/shard_map/ppermute | solution.py:17
  24.3 12.3 %copy-start.14 = (pred[8]{0:T(512)(128)(4,1)}, pred[8]{0:T(512)(128)(4,1)S(1)}, u32[]{:S(2)}) copy-start(pred[8]{0:T(512)(128)(4,1)S(1)} %fusion.48) | copy-start | bytes 28
  24.3 12.3 %copy-start.15 = (pred[8]{0:T(512)(128)(4,1)}, pred[8]{0:T(512)(128)(4,1)S(1)}, u32[]{:S(2)}) copy-start(pred[8]{0:T(512)(128)(4,1)S(1)} %compare_not_fusion) | copy-start | bytes 28
  34.7 53.2 %collective-permute-start = (bf16[2,128,1024]{1,2,0:T(8,128)(2,1)S(1)}, bf16[2,128,1024]{1,2,0:T(8,128)(2,1)}, u32[]{:S(2)}, u32[]{:S(2)}) collective-permute-start(bf16[2,128,1024]{1,2,0:T(8,128)(2,1)S(1)} %pad_maximum_fusion), channel_id=1, source_target_pairs={{0,4},{4,8},{8,12},{12,16},{16,20},{20,24},{24,28},{28,32},{32,36}... | collective-permute-start | bytes 1572872 | tf_op jit(solution)/shard_map/ppermute | solution.py:17
  89.2 1.0 copy-start.6
  89.2 1.0 copy-start.7
  90.3 3.8 %copy-start.1 = (bf16[2,8,128,8,128]{4,2,1,3,0:T(8,128)(2,1)}, bf16[2,8,128,8,128]{4,2,1,3,0:T(8,128)(2,1)S(1)}, u32[]{:S(2)}) copy-start(bf16[2,8,128,8,128]{4,2,1,3,0:T(8,128)(2,1)S(1)} %maximum_dynamic-update-slice_fusion) | copy-start | bytes 12582916
  90.3 2.0 copy-start.12
  94.1 3.7 %copy-start.5 = (bf16[128,1024]{1,0:T(8,128)(2,1)S(1)}, bf16[128,1024]{1,0:T(8,128)(2,1)}, u32[]{:S(2)}) copy-start(bf16[128,1024]{1,0:T(8,128)(2,1)} %param.16) | copy-start | bytes 786436
  96.4 13.7 %copy-start.13 = (pred[8,128,128]{2,1,0:T(8,128)(4,1)S(1)}, pred[8,128,128]{2,1,0:T(8,128)(4,1)}, u32[]{:S(2)}) copy-start(pred[8,128,128]{2,1,0:T(8,128)(4,1)} %or_and_fusion) | copy-start | bytes 393220
  113.4 18.7 %copy-start.3 = (bf16[8,8,128,128]{3,2,1,0:T(8,128)(2,1)}, bf16[8,8,128,128]{3,2,1,0:T(8,128)(2,1)S(1)}, u32[]{:S(2)}) copy-start(bf16[8,8,128,128]{3,2,1,0:T(8,128)(2,1)S(1)} %get-tuple-element.339) | copy-start | bytes 6291460
  115.6 18.9 %copy-start.4 = (bf16[8,8,128,128]{3,2,1,0:T(8,128)(2,1)}, bf16[8,8,128,128]{3,2,1,0:T(8,128)(2,1)S(1)}, u32[]{:S(2)}) copy-start(bf16[8,8,128,128]{3,2,1,0:T(8,128)(2,1)S(1)} %multiply_convert_fusion) | copy-start | bytes 6291460
  118.2 16.4 %copy-start.2 = (bf16[2,8,128,8,128]{4,2,1,3,0:T(8,128)(2,1)S(1)}, bf16[2,8,128,8,128]{4,2,1,3,0:T(8,128)(2,1)}, u32[]{:S(2)}) copy-start(bf16[2,8,128,8,128]{4,2,1,3,0:T(8,128)(2,1)} %copy-done.1) | copy-start | bytes 12582916
  118.6 14.7 %collective-permute-start.6 = (bf16[2,1,128,8,128]{2,4,3,1,0:T(8,128)(2,1)S(1)}, bf16[2,1,128,8,128]{2,4,3,1,0:T(8,128)(2,1)S(1)}, u32[]{:S(2)}, u32[]{:S(2)}) collective-permute-start(bf16[2,1,128,8,128]{2,4,3,1,0:T(8,128)(2,1)S(1)} %pad_maximum_fusion.1), channel_id=1, source_target_pairs={{4,0},{8,4},{12,8},{16,12},{20,16},{24,20},{28,24},{32,28},{36,32}... | collective-permute-start | bytes 1572872 | tf_op jit(solution)/shard_map/ppermute | solution.py:17
  121.6 28.3 %collective-permute-start.7 = (bf16[2,1,128,8,128]{2,4,3,1,0:T(8,128)(2,1)}, bf16[2,1,128,8,128]{2,4,3,1,0:T(8,128)(2,1)S(1)}, u32[]{:S(2)}, u32[]{:S(2)}) collective-permute-start(bf16[2,1,128,8,128]{2,4,3,1,0:T(8,128)(2,1)} %pad_maximum_fusion.2), channel_id=1, source_target_pairs={{8,0},{12,4},{16,8},{20,12},{24,16},{28,20},{32,24},{36,28},{40,32... | collective-permute-start | bytes 1572872 | tf_op jit(solution)/shard_map/ppermute | solution.py:17
  124.4 36.8 %collective-permute-start.8 = (bf16[2,1,128,8,128]{2,4,3,1,0:T(8,128)(2,1)}, bf16[2,1,128,8,128]{2,4,3,1,0:T(8,128)(2,1)S(1)}, u32[]{:S(2)}, u32[]{:S(2)}) collective-permute-start(bf16[2,1,128,8,128]{2,4,3,1,0:T(8,128)(2,1)} %pad_maximum_fusion.3), channel_id=1, source_target_pairs={{16,0},{20,4},{24,8},{28,12},{32,16},{36,20},{40,24},{44,28},{48,3... | collective-permute-start | bytes 1572872 | tf_op jit(solution)/shard_map/ppermute | solution.py:17
  127.1 57.4 %collective-permute-start.9 = (bf16[2,1,128,8,128]{2,4,3,1,0:T(8,128)(2,1)}, bf16[2,1,128,8,128]{2,4,3,1,0:T(8,128)(2,1)S(1)}, u32[]{:S(2)}, u32[]{:S(2)}) collective-permute-start(bf16[2,1,128,8,128]{2,4,3,1,0:T(8,128)(2,1)} %pad_maximum_fusion.4), channel_id=1, source_target_pairs={{32,0},{36,4},{40,8},{44,12},{48,16},{52,20},{56,24},{60,28},{64,3... | collective-permute-start | bytes 1572872 | tf_op jit(solution)/shard_map/ppermute | solution.py:17
  129.9 95.2 %collective-permute-start.10 = (bf16[2,1,128,8,128]{2,4,3,1,0:T(8,128)(2,1)}, bf16[2,1,128,8,128]{2,4,3,1,0:T(8,128)(2,1)S(1)}, u32[]{:S(2)}, u32[]{:S(2)}) collective-permute-start(bf16[2,1,128,8,128]{2,4,3,1,0:T(8,128)(2,1)} %pad_maximum_fusion.5), channel_id=1, source_target_pairs={{64,0},{68,4},{72,8},{76,12},{80,16},{84,20},{88,24},{92,28},{96,3... | collective-permute-start | bytes 1572872 | tf_op jit(solution)/shard_map/ppermute | solution.py:17
  133.3 91.8 %collective-permute-start.11 = (bf16[2,1,128,8,128]{2,4,3,1,0:T(8,128)(2,1)}, bf16[2,1,128,8,128]{2,4,3,1,0:T(8,128)(2,1)}, u32[]{:S(2)}, u32[]{:S(2)}) collective-permute-start(bf16[2,1,128,8,128]{2,4,3,1,0:T(8,128)(2,1)} %pad_maximum_fusion.6), channel_id=1, source_target_pairs={{128,0},{132,4},{136,8},{140,12},{144,16},{148,20},{152,24},{156,2... | collective-permute-start | bytes 1572872 | tf_op jit(solution)/shard_map/ppermute | solution.py:17
  (4 other events, 3.2 us)
where the time goes:
time: 230 us; the launch traced here: 228 us
  waiting for transfers between devices  132 us (57%)
  starting transfers between devices  33.4 us (15%)
  local copies, waits for them, and re-layouts  25.3 us (11%)
  matrix products  15.2 us (7%)
  blocking collectives  10.9 us (5%)
  other arithmetic  10.8 us (5%)
    ppermute x12, waiting for transfers between devices, shifted(): return lax.ppermute(block, axis, route)  132 us
    ppermute x12, starting transfers between devices, shifted(): return lax.ppermute(block, axis, route)  33.4 us
    psum x1, blocking collectives, shards(): square_sum = lax.psum(jnp.sum(attn_wide * attn_wide, axis=1), 'head')  10.9 us
    unnamed x46, local copies, waits for them, and re-layouts  10.8 us
    another operation x6, local copies, waits for them, and re-layouts, shards(): pair_kv = jnp.stack(gathered, axis=1)  7.87 us
  transfers between devices with their start and end apart: 12, of which 10 were waited for; matrix products, arithmetic and copies ran while one was open for 10% of the time, Pallas kernels for 0%

commit v1 on v0

--- a/solution.py
+++ b/solution.py
@@ -124,7 +124,7 @@
         "bhqsk,bskhd->bqhd", prob_stack, value_stack, preferred_element_type=jnp.float32
     ).astype(jnp.bfloat16)
     attn_wide = attention.reshape(tokens_here, heads_here * HD).astype(jnp.float32)
-    square_sum = lax.psum(jnp.sum(attn_wide * attn_wide, axis=1), "head")
+    square_sum = jnp.sum(lax.all_gather(jnp.sum(attn_wide * attn_wide, axis=1), "head"), axis=0)
     inverse = lax.rsqrt(square_sum / WIDTH + EPSILON)
     normed = (attn_wide * inverse[:, None]).astype(jnp.bfloat16)
     upstream_wide = upstream.astype(jnp.float32)

time: 230 us -> 237 us (1.030)
  blocking collectives: 10.9 us -> 17.8 us
    all_gather x0 -> x1, blocking collectives: none -> 7.09 us  [shards(): lax.all_gather(jnp.sum(attn_wide * attn_wide, axis=1), 'head')]
where the time goes in v1:
time: 237 us; the launch traced here: 235 us
  waiting for transfers between devices  132 us (56%)
  starting transfers between devices  33.4 us (14%)
  local copies, waits for them, and re-layouts  25.2 us (11%)
  blocking collectives  17.8 us (8%)
  matrix products  15.3 us (6%)
  other arithmetic  10.8 us (5%)
    ppermute x12, waiting for transfers between devices, shifted(): return lax.ppermute(block, axis, route)  132 us
    ppermute x12, starting transfers between devices, shifted(): return lax.ppermute(block, axis, route)  33.4 us
    unnamed x46, local copies, waits for them, and re-layouts  10.8 us
    psum x1, blocking collectives, shards(): cross_term = lax.psum(jnp.sum(upstream_wide * attn_wide, axis=1), 'head')  10.7 us
    another operation x6, local copies, waits for them, and re-layouts, shards(): pair_kv = jnp.stack(gathered, axis=1)  7.87 us
    all_gather x1, blocking collectives, shards(): lax.all_gather(jnp.sum(attn_wide * attn_wide, axis=1), 'head')  7.09 us
  transfers between devices with their start and end apart: 12, of which 10 were waited for; matrix products, arithmetic and copies ran while one was open for 10% of the time, Pallas kernels for 0%

profile of v1, /device:TPU:64, one launch (start us, length us, event | category | flops | bytes accessed | tf_op | source)
XLA Modules:
  0.0 235.4 jit_solution(16415817316279422817)
XLA Ops:
  3.0 8.1 %collective-permute-start.5 = (bf16[2,128,1024]{1,2,0:T(8,128)(2,1)S(1)}, bf16[2,128,1024]{1,2,0:T(8,128)(2,1)}, u32[]{:S(2)}, u32[]{:S(2)}) collective-permute-start(bf16[2,128,1024]{1,2,0:T(8,128)(2,1)S(1)} %pad_maximum_fusion), channel_id=1, source_target_pairs={{0,128},{4,132},{8,136},{12,140},{16,144},{20,148},{24,152},{28,15... | collective-permute-start | bytes 1572872 | tf_op jit(solution)/shard_map/ppermute | solution.py:17
  11.1 1.9 collective-permute-start.4
  13.0 2.9 %collective-permute-start.3 = (bf16[2,128,1024]{1,2,0:T(8,128)(2,1)S(1)}, bf16[2,128,1024]{1,2,0:T(8,128)(2,1)S(1)}, u32[]{:S(2)}, u32[]{:S(2)}) collective-permute-start(bf16[2,128,1024]{1,2,0:T(8,128)(2,1)S(1)} %pad_maximum_fusion), channel_id=1, source_target_pairs={{0,32},{4,36},{8,40},{12,44},{16,48},{20,52},{24,56},{28,60},{32,6... | collective-permute-start | bytes 1572872 | tf_op jit(solution)/shard_map/ppermute | solution.py:17
  15.9 4.9 %collective-permute-start.2 = (bf16[2,128,1024]{1,2,0:T(8,128)(2,1)S(1)}, bf16[2,128,1024]{1,2,0:T(8,128)(2,1)S(1)}, u32[]{:S(2)}, u32[]{:S(2)}) collective-permute-start(bf16[2,128,1024]{1,2,0:T(8,128)(2,1)S(1)} %pad_maximum_fusion), channel_id=1, source_target_pairs={{0,16},{4,20},{8,24},{12,28},{16,32},{20,36},{24,40},{28,44},{32,4... | collective-permute-start | bytes 1572872 | tf_op jit(solution)/shard_map/ppermute | solution.py:17
  20.9 2.5 %collective-permute-start.1 = (bf16[2,128,1024]{1,2,0:T(8,128)(2,1)S(1)}, bf16[2,128,1024]{1,2,0:T(8,128)(2,1)S(1)}, u32[]{:S(2)}, u32[]{:S(2)}) collective-permute-start(bf16[2,128,1024]{1,2,0:T(8,128)(2,1)S(1)} %pad_maximum_fusion), channel_id=1, source_target_pairs={{0,8},{4,12},{8,16},{12,20},{16,24},{20,28},{24,32},{28,36},{32,40... | collective-permute-start | bytes 1572872 | tf_op jit(solution)/shard_map/ppermute | solution.py:17
  24.3 10.3 %collective-permute-done.5 = bf16[2,128,1024]{1,2,0:T(8,128)(2,1)} collective-permute-done((bf16[2,128,1024]{1,2,0:T(8,128)(2,1)S(1)}, bf16[2,128,1024]{1,2,0:T(8,128)(2,1)}, u32[]{:S(2)}, u32[]{:S(2)}) %collective-permute-start.5) | collective-permute-done | bytes 524320 | tf_op jit(solution)/shard_map/ppermute | solution.py:17
  34.7 1.9 collective-permute-start
  44.5 11.9 %collective-permute-done.4 = bf16[2,128,1024]{1,2,0:T(8,128)(2,1)S(1)} collective-permute-done((bf16[2,128,1024]{1,2,0:T(8,128)(2,1)S(1)}, bf16[2,128,1024]{1,2,0:T(8,128)(2,1)S(1)}, u32[]{:S(2)}, u32[]{:S(2)}) %collective-permute-start.4) | collective-permute-done | bytes 524320 | tf_op jit(solution)/shard_map/ppermute | solution.py:17
  58.4 8.1 %collective-permute-done.3 = bf16[2,128,1024]{1,2,0:T(8,128)(2,1)S(1)} collective-permute-done((bf16[2,128,1024]{1,2,0:T(8,128)(2,1)S(1)}, bf16[2,128,1024]{1,2,0:T(8,128)(2,1)S(1)}, u32[]{:S(2)}, u32[]{:S(2)}) %collective-permute-start.3) | collective-permute-done | bytes 524320 | tf_op jit(solution)/shard_map/ppermute | solution.py:17
  68.7 2.5 %collective-permute-done.2 = bf16[2,128,1024]{1,2,0:T(8,128)(2,1)S(1)} collective-permute-done((bf16[2,128,1024]{1,2,0:T(8,128)(2,1)S(1)}, bf16[2,128,1024]{1,2,0:T(8,128)(2,1)S(1)}, u32[]{:S(2)}, u32[]{:S(2)}) %collective-permute-start.2) | collective-permute-done | bytes 524320 | tf_op jit(solution)/shard_map/ppermute | solution.py:17
  73.3 9.0 %collective-permute-done.1 = bf16[2,128,1024]{1,2,0:T(8,128)(2,1)S(1)} collective-permute-done((bf16[2,128,1024]{1,2,0:T(8,128)(2,1)S(1)}, bf16[2,128,1024]{1,2,0:T(8,128)(2,1)S(1)}, u32[]{:S(2)}, u32[]{:S(2)}) %collective-permute-start.1) | collective-permute-done | bytes 524320 | tf_op jit(solution)/shard_map/ppermute | solution.py:17
  84.3 3.5 %collective-permute-done = bf16[2,128,1024]{1,2,0:T(8,128)(2,1)} collective-permute-done((bf16[2,128,1024]{1,2,0:T(8,128)(2,1)S(1)}, bf16[2,128,1024]{1,2,0:T(8,128)(2,1)}, u32[]{:S(2)}, u32[]{:S(2)}) %collective-permute-start) | collective-permute-done | bytes 524320 | tf_op jit(solution)/shard_map/ppermute | solution.py:17
  90.3 2.0 slice_bitcast_fusion.1
  94.1 2.4 %multiply_reduce_fusion = (f32[128]{0:T(128)S(1)}, f32[8,128,128]{2,1,0:T(8,128)}) fusion(f32[8,8,128,128]{3,2,1,0:T(8,128)S(1)} %get-tuple-element.334, f32[8,128]{1,0:T(8,128)S(1)} %log_add_fusion, pred[128,8,128]{0,2,1:T(8,128)(4,1)S(1)} %and_bitcast_fusion, bf16[2,8,128,8,128]{4,2,1,3,0:T(8,128)(2,1)S(1)} %maximum_dynamic-update-slice_fusion), kind=kOutput, calls=%fused_computation.76 | convolution fusion | flops 273153920 | bytes 6951424 | tf_op jit(solution)/shard_map/bhqsk,bskhd->bqhd/dot_general | solution.py:123
  97.9 10.7 %psum.7 = f32[128]{0:T(128)S(1)} all-reduce(f32[128]{0:T(128)S(1)} %fusion.45), channel_id=1, replica_groups=mesh['ctx'=64,'head'=4] {'head'}, use_global_device_ids=true, to_apply=%region_5.6 | all-reduce | flops 128 | bytes 1024 | tf_op jit(solution)/shard_map/psum | solution.py:131
  108.6 7.1 %all-gather.1 = f32[4,1,128]{2,1,0:T(1,128)S(1)} all-gather(f32[1,1,128]{2,1,0:T(1,128)S(1)} %bitcast.289), channel_id=2, replica_groups=mesh['ctx'=64,'head'=4] {'head'}, dimensions={0}, use_global_device_ids=true | all-gather | bytes 2560 | tf_op jit(solution)/shard_map/all_gather | solution.py:127
  117.1 3.3 %fusion.3 = (bf16[8,8,128,128]{3,2,1,0:T(8,128)(2,1)S(1)}, f32[8,8,128,128]{2,3,1,0:T(8,128)S(1)}) fusion(f32[8,128]{1,0:T(8,128)S(1)} %log_add_fusion, pred[8,128,128]{2,1,0:T(8,128)(4,1)S(1)} %copy-done.13, bf16[128,8,128]{2,0,1:T(8,128)(2,1)} %copy_bitcast_fusion.1, bf16[8,128,8,128]{3,1,0,2:T(8,128)(2,1)} %get-tuple-element.325), kind=kOutput, calls=%fused_computation.8 | convolution fusion | flops 272629760 | bytes 8785920 | tf_op jit(solution)/shard_map/pqhd,pkhd->phqk/dot_general | solution.py:42
  120.4 2.2 multiply_convert_fusion
  125.5 2.2 collective-permute-start.6
  128.5 1.9 collective-permute-start.7
  145.6 11.2 %collective-permute-done.7 = bf16[2,1,128,8,128]{2,4,3,1,0:T(8,128)(2,1)S(1)} collective-permute-done((bf16[2,1,128,8,128]{2,4,3,1,0:T(8,128)(2,1)}, bf16[2,1,128,8,128]{2,4,3,1,0:T(8,128)(2,1)S(1)}, u32[]{:S(2)}, u32[]{:S(2)}) %collective-permute-start.7) | collective-permute-done | bytes 524320 | tf_op jit(solution)/shard_map/ppermute | solution.py:17
  156.8 11.2 %collective-permute-done.8 = bf16[2,1,128,8,128]{2,4,3,1,0:T(8,128)(2,1)S(1)} collective-permute-done((bf16[2,1,128,8,128]{2,4,3,1,0:T(8,128)(2,1)}, bf16[2,1,128,8,128]{2,4,3,1,0:T(8,128)(2,1)S(1)}, u32[]{:S(2)}, u32[]{:S(2)}) %collective-permute-start.8) | collective-permute-done | bytes 524320 | tf_op jit(solution)/shard_map/ppermute | solution.py:17
  168.1 23.4 %collective-permute-done.9 = bf16[2,1,128,8,128]{2,4,3,1,0:T(8,128)(2,1)S(1)} collective-permute-done((bf16[2,1,128,8,128]{2,4,3,1,0:T(8,128)(2,1)}, bf16[2,1,128,8,128]{2,4,3,1,0:T(8,128)(2,1)S(1)}, u32[]{:S(2)}, u32[]{:S(2)}) %collective-permute-start.9) | collective-permute-done | bytes 524320 | tf_op jit(solution)/shard_map/ppermute | solution.py:17
  191.5 40.6 %collective-permute-done.10 = bf16[2,1,128,8,128]{2,4,3,1,0:T(8,128)(2,1)S(1)} collective-permute-done((bf16[2,1,128,8,128]{2,4,3,1,0:T(8,128)(2,1)}, bf16[2,1,128,8,128]{2,4,3,1,0:T(8,128)(2,1)S(1)}, u32[]{:S(2)}, u32[]{:S(2)}) %collective-permute-start.10) | collective-permute-done | bytes 524320 | tf_op jit(solution)/shard_map/ppermute | solution.py:17
  (103 shorter events, 48.4 us)
Async XLA Ops:
  0.6 41.8 %copy-start = (bf16[128,1024]{1,0:T(8,128)(2,1)S(1)}, bf16[128,1024]{1,0:T(8,128)(2,1)}, u32[]{:S(2)}) copy-start(bf16[128,1024]{1,0:T(8,128)(2,1)} %param.12) | copy-start | bytes 786436
  3.0 31.7 %collective-permute-start.5 = (bf16[2,128,1024]{1,2,0:T(8,128)(2,1)S(1)}, bf16[2,128,1024]{1,2,0:T(8,128)(2,1)}, u32[]{:S(2)}, u32[]{:S(2)}) collective-permute-start(bf16[2,128,1024]{1,2,0:T(8,128)(2,1)S(1)} %pad_maximum_fusion), channel_id=1, source_target_pairs={{0,128},{4,132},{8,136},{12,140},{16,144},{20,148},{24,152},{28,15... | collective-permute-start | bytes 1572872 | tf_op jit(solution)/shard_map/ppermute | solution.py:17
  11.1 45.3 %collective-permute-start.4 = (bf16[2,128,1024]{1,2,0:T(8,128)(2,1)S(1)}, bf16[2,128,1024]{1,2,0:T(8,128)(2,1)S(1)}, u32[]{:S(2)}, u32[]{:S(2)}) collective-permute-start(bf16[2,128,1024]{1,2,0:T(8,128)(2,1)S(1)} %pad_maximum_fusion), channel_id=1, source_target_pairs={{0,64},{4,68},{8,72},{12,76},{16,80},{20,84},{24,88},{28,92},{32,9... | collective-permute-start | bytes 1572872 | tf_op jit(solution)/shard_map/ppermute | solution.py:17
  13.0 53.6 %collective-permute-start.3 = (bf16[2,128,1024]{1,2,0:T(8,128)(2,1)S(1)}, bf16[2,128,1024]{1,2,0:T(8,128)(2,1)S(1)}, u32[]{:S(2)}, u32[]{:S(2)}) collective-permute-start(bf16[2,128,1024]{1,2,0:T(8,128)(2,1)S(1)} %pad_maximum_fusion), channel_id=1, source_target_pairs={{0,32},{4,36},{8,40},{12,44},{16,48},{20,52},{24,56},{28,60},{32,6... | collective-permute-start | bytes 1572872 | tf_op jit(solution)/shard_map/ppermute | solution.py:17
  15.9 55.2 %collective-permute-start.2 = (bf16[2,128,1024]{1,2,0:T(8,128)(2,1)S(1)}, bf16[2,128,1024]{1,2,0:T(8,128)(2,1)S(1)}, u32[]{:S(2)}, u32[]{:S(2)}) collective-permute-start(bf16[2,128,1024]{1,2,0:T(8,128)(2,1)S(1)} %pad_maximum_fusion), channel_id=1, source_target_pairs={{0,16},{4,20},{8,24},{12,28},{16,32},{20,36},{24,40},{28,44},{32,4... | collective-permute-start | bytes 1572872 | tf_op jit(solution)/shard_map/ppermute | solution.py:17
  20.9 61.4 %collective-permute-start.1 = (bf16[2,128,1024]{1,2,0:T(8,128)(2,1)S(1)}, bf16[2,128,1024]{1,2,0:T(8,128)(2,1)S(1)}, u32[]{:S(2)}, u32[]{:S(2)}) collective-permute-start(bf16[2,128,1024]{1,2,0:T(8,128)(2,1)S(1)} %pad_maximum_fusion), channel_id=1, source_target_pairs={{0,8},{4,12},{8,16},{12,20},{16,24},{20,28},{24,32},{28,36},{32,40... | collective-permute-start | bytes 1572872 | tf_op jit(solution)/shard_map/ppermute | solution.py:17
  24.3 12.3 %copy-start.14 = (pred[8]{0:T(512)(128)(4,1)}, pred[8]{0:T(512)(128)(4,1)S(1)}, u32[]{:S(2)}) copy-start(pred[8]{0:T(512)(128)(4,1)S(1)} %fusion.48) | copy-start | bytes 28
  24.3 12.3 %copy-start.15 = (pred[8]{0:T(512)(128)(4,1)}, pred[8]{0:T(512)(128)(4,1)S(1)}, u32[]{:S(2)}) copy-start(pred[8]{0:T(512)(128)(4,1)S(1)} %compare_not_fusion) | copy-start | bytes 28
  34.7 53.2 %collective-permute-start = (bf16[2,128,1024]{1,2,0:T(8,128)(2,1)S(1)}, bf16[2,128,1024]{1,2,0:T(8,128)(2,1)}, u32[]{:S(2)}, u32[]{:S(2)}) collective-permute-start(bf16[2,128,1024]{1,2,0:T(8,128)(2,1)S(1)} %pad_maximum_fusion), channel_id=1, source_target_pairs={{0,4},{4,8},{8,12},{12,16},{16,20},{20,24},{24,28},{28,32},{32,36}... | collective-permute-start | bytes 1572872 | tf_op jit(solution)/shard_map/ppermute | solution.py:17
  89.2 1.0 copy-start.6
  89.2 1.0 copy-start.7
  90.3 3.7 %copy-start.1 = (bf16[2,8,128,8,128]{4,2,1,3,0:T(8,128)(2,1)}, bf16[2,8,128,8,128]{4,2,1,3,0:T(8,128)(2,1)S(1)}, u32[]{:S(2)}) copy-start(bf16[2,8,128,8,128]{4,2,1,3,0:T(8,128)(2,1)S(1)} %maximum_dynamic-update-slice_fusion) | copy-start | bytes 12582916
  90.3 2.0 copy-start.12
  94.0 3.7 %copy-start.5 = (bf16[128,1024]{1,0:T(8,128)(2,1)S(1)}, bf16[128,1024]{1,0:T(8,128)(2,1)}, u32[]{:S(2)}) copy-start(bf16[128,1024]{1,0:T(8,128)(2,1)} %param.16) | copy-start | bytes 786436
  96.4 20.6 %copy-start.13 = (pred[8,128,128]{2,1,0:T(8,128)(4,1)S(1)}, pred[8,128,128]{2,1,0:T(8,128)(4,1)}, u32[]{:S(2)}) copy-start(pred[8,128,128]{2,1,0:T(8,128)(4,1)} %or_and_fusion) | copy-start | bytes 393220
  120.4 18.6 %copy-start.3 = (bf16[8,8,128,128]{3,2,1,0:T(8,128)(2,1)}, bf16[8,8,128,128]{3,2,1,0:T(8,128)(2,1)S(1)}, u32[]{:S(2)}) copy-start(bf16[8,8,128,128]{3,2,1,0:T(8,128)(2,1)S(1)} %get-tuple-element.337) | copy-start | bytes 6291460
  122.6 18.9 %copy-start.4 = (bf16[8,8,128,128]{3,2,1,0:T(8,128)(2,1)}, bf16[8,8,128,128]{3,2,1,0:T(8,128)(2,1)S(1)}, u32[]{:S(2)}) copy-start(bf16[8,8,128,128]{3,2,1,0:T(8,128)(2,1)S(1)} %multiply_convert_fusion) | copy-start | bytes 6291460
  125.1 16.3 %copy-start.2 = (bf16[2,8,128,8,128]{4,2,1,3,0:T(8,128)(2,1)S(1)}, bf16[2,8,128,8,128]{4,2,1,3,0:T(8,128)(2,1)}, u32[]{:S(2)}) copy-start(bf16[2,8,128,8,128]{4,2,1,3,0:T(8,128)(2,1)} %copy-done.1) | copy-start | bytes 12582916
  125.5 14.7 %collective-permute-start.6 = (bf16[2,1,128,8,128]{2,4,3,1,0:T(8,128)(2,1)S(1)}, bf16[2,1,128,8,128]{2,4,3,1,0:T(8,128)(2,1)S(1)}, u32[]{:S(2)}, u32[]{:S(2)}) collective-permute-start(bf16[2,1,128,8,128]{2,4,3,1,0:T(8,128)(2,1)S(1)} %pad_maximum_fusion.1), channel_id=1, source_target_pairs={{4,0},{8,4},{12,8},{16,12},{20,16},{24,20},{28,24},{32,28},{36,32}... | collective-permute-start | bytes 1572872 | tf_op jit(solution)/shard_map/ppermute | solution.py:17
  128.5 28.3 %collective-permute-start.7 = (bf16[2,1,128,8,128]{2,4,3,1,0:T(8,128)(2,1)}, bf16[2,1,128,8,128]{2,4,3,1,0:T(8,128)(2,1)S(1)}, u32[]{:S(2)}, u32[]{:S(2)}) collective-permute-start(bf16[2,1,128,8,128]{2,4,3,1,0:T(8,128)(2,1)} %pad_maximum_fusion.2), channel_id=1, source_target_pairs={{8,0},{12,4},{16,8},{20,12},{24,16},{28,20},{32,24},{36,28},{40,32... | collective-permute-start | bytes 1572872 | tf_op jit(solution)/shard_map/ppermute | solution.py:17
  131.3 36.8 %collective-permute-start.8 = (bf16[2,1,128,8,128]{2,4,3,1,0:T(8,128)(2,1)}, bf16[2,1,128,8,128]{2,4,3,1,0:T(8,128)(2,1)S(1)}, u32[]{:S(2)}, u32[]{:S(2)}) collective-permute-start(bf16[2,1,128,8,128]{2,4,3,1,0:T(8,128)(2,1)} %pad_maximum_fusion.3), channel_id=1, source_target_pairs={{16,0},{20,4},{24,8},{28,12},{32,16},{36,20},{40,24},{44,28},{48,3... | collective-permute-start | bytes 1572872 | tf_op jit(solution)/shard_map/ppermute | solution.py:17
  134.0 57.5 %collective-permute-start.9 = (bf16[2,1,128,8,128]{2,4,3,1,0:T(8,128)(2,1)}, bf16[2,1,128,8,128]{2,4,3,1,0:T(8,128)(2,1)S(1)}, u32[]{:S(2)}, u32[]{:S(2)}) collective-permute-start(bf16[2,1,128,8,128]{2,4,3,1,0:T(8,128)(2,1)} %pad_maximum_fusion.4), channel_id=1, source_target_pairs={{32,0},{36,4},{40,8},{44,12},{48,16},{52,20},{56,24},{60,28},{64,3... | collective-permute-start | bytes 1572872 | tf_op jit(solution)/shard_map/ppermute | solution.py:17
  136.8 95.3 %collective-permute-start.10 = (bf16[2,1,128,8,128]{2,4,3,1,0:T(8,128)(2,1)}, bf16[2,1,128,8,128]{2,4,3,1,0:T(8,128)(2,1)S(1)}, u32[]{:S(2)}, u32[]{:S(2)}) collective-permute-start(bf16[2,1,128,8,128]{2,4,3,1,0:T(8,128)(2,1)} %pad_maximum_fusion.5), channel_id=1, source_target_pairs={{64,0},{68,4},{72,8},{76,12},{80,16},{84,20},{88,24},{92,28},{96,3... | collective-permute-start | bytes 1572872 | tf_op jit(solution)/shard_map/ppermute | solution.py:17
  140.2 91.9 %collective-permute-start.11 = (bf16[2,1,128,8,128]{2,4,3,1,0:T(8,128)(2,1)}, bf16[2,1,128,8,128]{2,4,3,1,0:T(8,128)(2,1)}, u32[]{:S(2)}, u32[]{:S(2)}) collective-permute-start(bf16[2,1,128,8,128]{2,4,3,1,0:T(8,128)(2,1)} %pad_maximum_fusion.6), channel_id=1, source_target_pairs={{128,0},{132,4},{136,8},{140,12},{144,16},{148,20},{152,24},{156,2... | collective-permute-start | bytes 1572872 | tf_op jit(solution)/shard_map/ppermute | solution.py:17
  (4 other events, 3.1 us)
